TPU v7x, 32 devices: a whole 2x2x4 slice. The times are simulated.
32 devices in a mesh: elem: 8 (over z, x), band: 4 (over y, core).
Axes of the slice: x: 2, y: 2, z: 4, core: 2. Of those that a mesh axis runs over, the one named last changes fastest.
Arguments:
- crm_state: bfloat16 [8, 128, 6, 3840], P('elem', 'band'), may hold values from -6 to 6
- host_state: float32 [72, 8, 128], P(None, 'elem', 'band'), may hold values from -6 to 6
- kappa: float32 [8, 128], P('elem', 'band'), may hold values from 0.02 to 0.2
- substeps: int32 [8, 128], P('elem', 'band'), may hold values from 1 to 4, as said below
- coupling: float32 [6, 6], replicated, may hold values from -2.5 to 2.5
- level_map: float32 [60, 72], replicated, may hold values from -0.75 to 0.75
- field_scale: float32 [6], replicated, may hold values from 0.5 to 1.5
- back_map: float32 [72, 60], replicated, may hold values from -0.75 to 0.75
- back_weight: float32 [6], replicated, may hold values from -3 to 3
Outputs:
- crm_final: bfloat16 [8, 128, 6, 3840], P('elem', 'band')
- host_final: float32 [72, 8, 128], P(None, 'elem', 'band')
Inputs may be any that keep to these rules, and one draw needn't show every extreme that they name: Each aligned block of 1 x 32 columns (the columns of one device) draws a level from 1 to 4; each column of the block takes 1 plus a uniform integer modulo that level substeps. Column (0, 0) takes 4 substeps and column (0, 1) takes 1.
All inputs are finite; a program needn't handle non-finite values.
Results may differ from a plain program's by a relative error of at most 0.0055.
Values may be sent and summed in bfloat16 or wider, within the bound.
No kernel may reach another device: no remote copies, remote signals or barrier semaphores. Data moves between devices by JAX's collectives and lax.ppermute only.
A program may use at most 128 MiB of HBM per device.

v0:
```python
import jax
import jax.numpy as jnp
from jax import lax
from jax.experimental import pallas as pl
from jax.experimental.pallas import tpu as pltpu
from jax.sharding import PartitionSpec as P

FIELDS = 6
NZC = 60
NXC = 64
SUB = 4
WINDOWS = 2
LANES = 2 * NXC
COLS = 32
SIZE = 8
PAIR = 2 * SIZE
GROUPS = COLS // SIZE
QUARTER = NZC // 4
HALF_TILES = NZC // 4
CELLS = NZC * NXC
CHUNK = 3
CLOUD_STEP = 0.1
F32 = jnp.float32
BF16 = jnp.bfloat16
HIGHEST = lax.Precision.HIGHEST


def row_iota(*shape):
    return lax.broadcasted_iota(jnp.int32, shape, 0)


def lane_iota(*shape):
    return lax.broadcasted_iota(jnp.int32, shape, 1)


def column_of(row):
    square = jnp.broadcast_to(row, (COLS, COLS))
    eye = row_iota(COLS, COLS) == lane_iota(COLS, COLS)
    return jnp.sum(jnp.where(eye, square, 0.0), axis=1, keepdims=True)


def ranks(counts_row):
    rows = row_iota(COLS, COLS)
    lanes = lane_iota(COLS, COLS)
    along_lanes = jnp.broadcast_to(counts_row, (COLS, COLS))
    column = column_of(counts_row)
    along_rows = jnp.broadcast_to(column, (COLS, COLS))
    before = (along_lanes > along_rows) | ((along_lanes == along_rows) & (lanes < rows))
    rank_col = jnp.sum(jnp.where(before, 1.0, 0.0), axis=1, keepdims=True)
    after = (along_rows > along_lanes) | ((along_rows == along_lanes) & (rows < lanes))
    rank_row = jnp.sum(jnp.where(after, 1.0, 0.0), axis=0, keepdims=True)
    to_slot = jnp.where(jnp.broadcast_to(rank_row, (COLS, COLS)) == rows.astype(F32), 1.0, 0.0)
    to_column = jnp.where(jnp.broadcast_to(rank_col, (COLS, COLS)) == lanes.astype(F32), 1.0, 0.0)
    return to_slot, to_column, column


def hi_lo(value):
    hi = value.astype(BF16)
    rest = value - hi.astype(F32)
    mid = rest.astype(BF16)
    return hi, mid, (rest - mid.astype(F32)).astype(BF16)


def permuted(one_hot, value):
    total = None
    for part in hi_lo(value):
        term = jnp.dot(one_hot, part, preferred_element_type=F32)
        total = term if total is None else total + term
    return total


def quarter_of(level):
    part, place = divmod(level, QUARTER)
    half, sub = divmod(part, 2)
    return half, sub, place


def weighted(state, g, zi, weights):
    total = weights[0] * state[g, zi, 0]
    for f in range(1, FIELDS):
        total = total + weights[f] * state[g, zi, f]
    return total


def prepare_force(force, host_sorted, level_map, fscale, expand):
    mapped = lax.dot_general(
        host_sorted, level_map[...], (((1,), (1,)), ((), ())), precision=HIGHEST,
        preferred_element_type=F32,
    )
    mapped = jnp.concatenate([mapped, jnp.zeros((COLS, NXC - NZC), F32)], axis=1)
    hi = mapped.astype(BF16)
    lo = (mapped - hi.astype(F32)).astype(BF16)
    parts = jnp.concatenate([hi, lo], axis=0)
    for zi in range(QUARTER):
        both = jnp.dot(
            parts, expand[:, 2 * zi * LANES : 2 * (zi + 1) * LANES], preferred_element_type=F32
        )
        both = both[:COLS] + both[COLS:]
        for g in range(GROUPS):
            rows = both[g * SIZE : (g + 1) * SIZE]
            spread = jnp.concatenate([rows[:, :LANES], rows[:, LANES:]], axis=0)
            for f in range(FIELDS):
                force[g, zi, f] = fscale[f] * spread


def advance_window(state, force, counts16, most, edge, dmat, cmat):
    low = lane_iota(SIZE, LANES) < NXC

    def substep(turn, active):
        for g in range(active):
            step = jnp.where(counts16[g] > turn.astype(F32), CLOUD_STEP, 0.0)
            keep = 1.0 - 2.0 * step
            prev = []
            for f in range(FIELDS):
                first = state[g, 0, f]
                last = state[g, QUARTER - 1, f]
                edge[g, f] = jnp.concatenate(
                    [first[SIZE:], jnp.where(low, pltpu.roll(first[:SIZE], NXC, 1), 0.0)], axis=0
                )
                prev.append(
                    jnp.concatenate(
                        [jnp.where(low, 0.0, pltpu.roll(last[SIZE:], NXC, 1)), last[:SIZE]], axis=0
                    )
                )
            for start in range(0, QUARTER, CHUNK):
                places = range(start, start + CHUNK)
                flats = [state[g, zi].reshape(FIELDS * PAIR, LANES).astype(BF16) for zi in places]
                slopes = jnp.dot(
                    jnp.concatenate(flats, axis=0), dmat[...], preferred_element_type=F32
                )
                for i, zi in enumerate(places):
                    mixed = jnp.dot(cmat[...], flats[i], preferred_element_type=F32)
                    now = [state[g, zi, f] for f in range(FIELDS)]
                    news = []
                    for f in range(FIELDS):
                        rows = slice(f * PAIR, (f + 1) * PAIR)
                        here = (i * FIELDS + f) * PAIR
                        slope = slopes[here : here + PAIR]
                        after = edge[g, f] if zi == QUARTER - 1 else state[g, zi + 1, f]
                        change = (prev[f] + after) + (
                            now[0] * slope + (jnp.tanh(mixed[rows]) + force[g, zi, f])
                        )
                        news.append(keep * now[f] + step * change)
                    for f in range(FIELDS):
                        state[g, zi, f] = news[f]
                    prev = now

    def body(turn, carry):
        running = sum(jnp.where(most[g] > turn, 1, 0) for g in range(GROUPS))
        for active in range(1, GROUPS + 1):
            pl.when(running == active)(lambda active=active: substep(turn, active))
        return carry

    lax.fori_loop(0, most[0], body, 0)


def differences(state, sums, weights, diffs):
    for zi in range(QUARTER):
        changes = []
        for g in range(GROUPS):
            end = weighted(state, g, zi, weights)
            changes.append(end - sums[g, zi])
            sums[g, zi] = end
        for sub in range(2):
            rows = jnp.concatenate([c[sub * SIZE : (sub + 1) * SIZE] for c in changes], axis=0)
            place = 2 * zi + sub
            diffs[:, place * LANES : (place + 1) * LANES] = rows.astype(BF16)


def tendency(diffs, backx, to_column):
    both = jnp.dot(diffs[...], backx[...], preferred_element_type=F32)
    return permuted(to_column, both[:, :LANES] + both[:, LANES:])


def swapped_halves(low, one, two):
    outer = jnp.where(low, one, two)
    inner = pltpu.roll(jnp.where(low, two, one), NXC, 1)
    return jnp.where(low, outer, inner), jnp.where(low, inner, outer)


def cloud_kernel(
    cloud_in, own_in, band_a_in, elem_a_in, band_b_in, elem_b_in, counts_in, level_in, back_in, coup_in, fscale_in,
    bweight_in,
    cloud_out, host_out, aux_out,
    own, band_a, elem_a, band_b, elem_b, counts, level_map, back_t, coup, fscale, bweight,
    state, force, sums, edge, dmat, cmat, counts16, backx, diffs, most, expand,
    out_buf, cloud, host_buf, aux, sems,
):
    levels = host_out.shape[1]
    sources = (
        own_in, band_a_in, elem_a_in, band_b_in, elem_b_in, counts_in, level_in, back_in, coup_in, fscale_in,
        bweight_in,
    )
    places = (own, band_a, elem_a, band_b, elem_b, counts, level_map, back_t, coup, fscale, bweight)
    copies = [
        pltpu.make_async_copy(src, dst, sems.at[FIELDS + i])
        for i, (src, dst) in enumerate(zip(sources, places))
    ]
    for copy in copies:
        copy.start()
    loads = [
        pltpu.make_async_copy(cloud_in.at[f], cloud.at[f], sems.at[f]) for f in range(FIELDS)
    ]
    for copy in loads:
        copy.start()
    r, l = row_iota(LANES, LANES), lane_iota(LANES, LANES)
    same = (r // NXC) == (l // NXC)
    ahead = same & (r % NXC == (l + 1) % NXC)
    behind = same & (r % NXC == (l + NXC - 1) % NXC)
    dmat[...] = (jnp.where(behind, 0.5, 0.0) - jnp.where(ahead, 0.5, 0.0)).astype(BF16)
    r, l = row_iota(NXC, LANES), lane_iota(NXC, LANES)
    for zi in range(QUARTER):
        for sub in range(2):
            level = sub * QUARTER + zi
            level = jnp.where(l < NXC, level, level + 2 * QUARTER)
            part = slice((2 * zi + sub) * LANES, (2 * zi + sub + 1) * LANES)
            expand[:, part] = jnp.where(r == level, 1.0, 0.0).astype(BF16)
    for copy in copies:
        copy.wait()

    counts_row = counts[...].astype(F32)
    to_slot, to_column, column = ranks(counts_row)
    to_slot = to_slot.astype(BF16)
    to_column = to_column.astype(BF16)
    over = [jnp.sum(jnp.where(counts[...] > turn, 1, 0)) for turn in range(1, SUB)]
    for g in range(GROUPS):
        most[g] = 1 + sum(jnp.where(over_turn > g * SIZE, 1, 0) for over_turn in over)
    counts_sorted = jnp.dot(
        to_slot, jnp.broadcast_to(column, (COLS, LANES)).astype(BF16), preferred_element_type=F32
    )
    for g in range(GROUPS):
        rows = counts_sorted[g * SIZE : (g + 1) * SIZE]
        counts16[g] = jnp.concatenate([rows, rows], axis=0)
    weights = [bweight[f] for f in range(FIELDS)]

    r, l = row_iota(FIELDS * PAIR, FIELDS * PAIR), lane_iota(FIELDS * PAIR, FIELDS * PAIR)
    same = (r % PAIR) == (l % PAIR)
    mixer = jnp.zeros((FIELDS * PAIR, FIELDS * PAIR), F32)
    for f in range(FIELDS):
        for other in range(FIELDS):
            here = same & (r // PAIR == f) & (l // PAIR == other)
            mixer = jnp.where(here, coup[f, other], mixer)
    cmat[...] = mixer.astype(BF16)
    padding = jnp.zeros((1, LANES - levels), F32)
    for zi in range(QUARTER):
        for sub in range(2):
            for half in range(2):
                level = (2 * half + sub) * QUARTER + zi
                row = jnp.concatenate([back_t[level : level + 1, :], padding], axis=1) * (1.0 / NXC)
                hi = row.astype(BF16)
                lo = (row - hi.astype(F32)).astype(BF16)
                first = ((2 * zi + sub) * 2 + half) * NXC
                backx[first : first + NXC, :LANES] = jnp.broadcast_to(hi, (NXC, LANES))
                backx[first : first + NXC, LANES:] = jnp.broadcast_to(lo, (NXC, LANES))

    even = lax.rem(lax.axis_index("band"), 2) == 0
    north = jnp.where(even, band_a[...], band_b[...])
    south = jnp.where(even, band_b[...], band_a[...])
    host = own[:COLS]
    kap, kap_a, kap_b, kap_n, kap_s = (
        column_of(ref[COLS : COLS + 1, :COLS]) for ref in (own, elem_a, elem_b, north, south)
    )
    face_a = 0.5 * (kap + kap_a)
    face_b = 0.5 * (kap + kap_b)
    face_n = 0.5 * (kap + jnp.concatenate([kap[1:], kap_n[:1]], axis=0))
    face_s = 0.5 * (kap + jnp.concatenate([kap_s[COLS - 1 :], kap[:-1]], axis=0))
    spread = face_a * (elem_a[:COLS] - host) + face_b * (elem_b[:COLS] - host)
    spread = spread + face_n * (jnp.concatenate([host[1:], north[0:1]], axis=0) - host)
    spread = spread + face_s * (
        jnp.concatenate([south[COLS - 1 : COLS], host[:-1]], axis=0) - host
    )

    prepare_force(force, permuted(to_slot, host), level_map, fscale, expand)

    low = lane_iota(COLS, LANES) < NXC
    for copy in loads:
        copy.wait()
    for f in range(FIELDS):
        for tile in range(HALF_TILES):
            near = slice(tile * LANES, (tile + 1) * LANES)
            far = slice((tile + HALF_TILES) * LANES, (tile + HALF_TILES + 1) * LANES)
            _, sub, place = quarter_of(2 * tile)
            _, sub2, place2 = quarter_of(2 * tile + 1)
            both = jnp.concatenate(swapped_halves(low, cloud[f, :, near], cloud[f, :, far]), axis=1)
            both = jnp.dot(to_slot, both, preferred_element_type=F32)
            for g in range(GROUPS):
                rows = both[g * SIZE : (g + 1) * SIZE]
                state[g, place, f, sub * SIZE : (sub + 1) * SIZE, :] = rows[:, :LANES]
                state[g, place2, f, sub2 * SIZE : (sub2 + 1) * SIZE, :] = rows[:, LANES:]
    for g in range(GROUPS):
        for zi in range(QUARTER):
            sums[g, zi] = weighted(state, g, zi, weights)

    advance_window(state, force, counts16, most, edge, dmat, cmat)
    differences(state, sums, weights, diffs)
    tend = tendency(diffs, backx, to_column)
    host = host + (tend[:, :levels] + spread)
    host_buf[...] = host
    sending = [pltpu.make_async_copy(host_buf, host_out, sems.at[0])]
    sending[0].start()
    prepare_force(force, permuted(to_slot, host), level_map, fscale, expand)
    advance_window(state, force, counts16, most, edge, dmat, cmat)
    for fields in (range(0, FIELDS // 2), range(FIELDS // 2, FIELDS)):
        for tile in range(HALF_TILES):
            near = slice(tile * LANES, (tile + 1) * LANES)
            far = slice((tile + HALF_TILES) * LANES, (tile + HALF_TILES + 1) * LANES)
            _, sub, place = quarter_of(2 * tile)
            _, sub2, place2 = quarter_of(2 * tile + 1)
            for f in fields:
                rows = jnp.concatenate(
                    [
                        jnp.concatenate(
                            [
                                state[g, place, f, sub * SIZE : (sub + 1) * SIZE, :],
                                state[g, place2, f, sub2 * SIZE : (sub2 + 1) * SIZE, :],
                            ],
                            axis=1,
                        )
                        for g in range(GROUPS)
                    ],
                    axis=0,
                )
                out = jnp.dot(to_column, rows.astype(BF16), preferred_element_type=F32).astype(BF16)
                one, two = swapped_halves(low, out[:, :LANES], out[:, LANES:])
                out_buf[f, :, near] = one
                out_buf[f, :, far] = two
        for f in fields:
            copy = pltpu.make_async_copy(out_buf.at[f], cloud_out.at[f], sems.at[len(sending)])
            copy.start()
            sending.append(copy)
    differences(state, sums, weights, diffs)

    tend = tendency(diffs, backx, to_column)
    zero = jnp.zeros((1, levels), F32)
    base = host + (tend[:, :levels] - (face_a + face_b + face_n + face_s) * host)
    base = base + face_n * jnp.concatenate([host[1:], zero], axis=0)
    base = base + face_s * jnp.concatenate([zero, host[:-1]], axis=0)
    room = jnp.zeros((COLS, LANES - levels - 4), F32)
    aux[...] = jnp.concatenate([base, face_a, face_b, face_n, face_s, room], axis=1)
    copy = pltpu.make_async_copy(aux, aux_out, sems.at[len(sending)])
    copy.start()
    sending.append(copy)
    for copy in sending:
        copy.wait()


def host_kernel(aux, band_a, elem_a, band_b, elem_b, out):
    levels = out.shape[1]
    face_a, face_b, face_n, face_s = (aux[:, levels + i : levels + i + 1] for i in range(4))
    total = aux[:, :levels] + (face_a * elem_a[...] + face_b * elem_b[...])
    even = lax.rem(lax.axis_index("band"), 2) == 0
    north = jnp.where(even, band_a[0:1], band_b[0:1])
    south = jnp.where(even, band_b[COLS - 1 : COLS], band_a[COLS - 1 : COLS])
    rows = row_iota(*total.shape)
    total = total + jnp.where(rows == COLS - 1, face_n * north, 0.0)
    out[...] = total + jnp.where(rows == 0, face_s * south, 0.0)


def neighbours(block):
    found = []
    for odd in range(2):
        for axis in ("band", "elem"):
            count = lax.axis_size(axis)
            pairs = [(i, (i + 1 - 2 * ((i + odd) % 2)) % count) for i in range(count)]
            found.append(lax.ppermute(block, axis, pairs))
    return found


VMEM = pl.BlockSpec(memory_space=pltpu.VMEM)
SMEM = pl.BlockSpec(memory_space=pltpu.SMEM)
HBM = pl.BlockSpec(memory_space=pl.ANY)
STATE = (GROUPS, QUARTER, FIELDS, PAIR, LANES)


def body(
    crm_state, host_state, kappa, substeps, coupling, level_map, field_scale, back_map, back_weight
):
    levels = host_state.shape[0]
    cloud = jnp.transpose(crm_state[0], (1, 0, 2))
    host = jnp.transpose(host_state[:, 0, :], (1, 0))
    own = jnp.concatenate([host, jnp.pad(kappa, ((0, 0), (0, levels - COLS)))], axis=0)
    near = neighbours(own)
    cloud_out, host, aux = pl.pallas_call(
        cloud_kernel,
        out_shape=(
            jax.ShapeDtypeStruct(cloud.shape, BF16),
            jax.ShapeDtypeStruct((COLS, levels), F32),
            jax.ShapeDtypeStruct((COLS, LANES), F32),
        ),
        in_specs=[HBM] * 12,
        out_specs=(HBM,) * 3,
        scratch_shapes=[pltpu.VMEM(own.shape, F32)] * 5
        + [
            pltpu.VMEM((1, COLS), jnp.int32),
            pltpu.VMEM((NZC, levels), F32),
            pltpu.VMEM((NZC, levels), F32),
            pltpu.SMEM((FIELDS, FIELDS), F32),
            pltpu.SMEM((FIELDS,), F32),
            pltpu.SMEM((FIELDS,), F32),
            pltpu.VMEM(STATE, F32),
            pltpu.VMEM(STATE, F32),
            pltpu.VMEM((GROUPS, QUARTER, PAIR, LANES), F32),
            pltpu.VMEM((GROUPS, FIELDS, PAIR, LANES), F32),
            pltpu.VMEM((LANES, LANES), BF16),
            pltpu.VMEM((FIELDS * PAIR, FIELDS * PAIR), BF16),
            pltpu.VMEM((GROUPS, PAIR, LANES), F32),
            pltpu.VMEM((CELLS, 2 * LANES), BF16),
            pltpu.VMEM((COLS, CELLS), BF16),
            pltpu.SMEM((GROUPS,), jnp.int32),
            pltpu.VMEM((NXC, CELLS), BF16),
            pltpu.VMEM((FIELDS, COLS, CELLS), BF16),
            pltpu.VMEM((FIELDS, COLS, CELLS), BF16),
            pltpu.VMEM((COLS, levels), F32),
            pltpu.VMEM((COLS, LANES), F32),
            pltpu.SemaphoreType.DMA((FIELDS + 11,)),
        ],
        compiler_params=pltpu.CompilerParams(vmem_limit_bytes=56 * 1024 * 1024),
        name="cloud_windows",
    )(cloud, own, *near, substeps, level_map, back_map.T, coupling, field_scale, back_weight)
    host = pl.pallas_call(
        host_kernel,
        out_shape=jax.ShapeDtypeStruct((COLS, levels), F32),
        in_specs=[VMEM] * 5,
        out_specs=VMEM,
        compiler_params=pltpu.CompilerParams(vmem_limit_bytes=1024 * 1024),
        name="host_section",
    )(aux, *neighbours(host))
    crm_final = jnp.transpose(cloud_out, (1, 0, 2))[None]
    host_final = jnp.transpose(host, (1, 0))[:, None, :]
    return (crm_final, host_final)


def solution(mesh):
    return jax.shard_map(
        body,
        mesh=mesh,
        in_specs=(
            P("elem", "band", None, None),
            P(None, "elem", "band"),
            P("elem", "band"),
            P("elem", "band"),
            P(),
            P(),
            P(),
            P(),
            P(),
        ),
        out_specs=(P("elem", "band", None, None), P(None, "elem", "band")),
        check_vma=False,
    )
```

profile of v0, /device:TPU:0, one launch (start us, length us, event | category | flops | bytes accessed | tf_op | source)
XLA Modules:
  0.0 31.6 jit_solution(2117642868631084612)
XLA Ops:
  0.6 0.7 %select_maximum_fusion.own_in = f32[33,72]{1,0:T(8,128)S(1)} fusion(f32[1,32]{1,0:T(1,128)} %param.11, f32[32,72]{1,0:T(8,128)} %bitcast.15), kind=kLoop, calls=%fused_computation | loop fusion | flops 7128 | bytes 18848 | tf_op jit(solution)/shard_map/concatenate | solution.py:381
  1.4 0.0 copy-start.1
  1.4 6.0 %collective-permute-start.3 = (f32[33,72]{1,0:T(8,128)S(1)}, f32[33,72]{1,0:T(8,128)S(1)}, u32[]{:S(2)}, u32[]{:S(2)}) collective-permute-start(f32[33,72]{1,0:T(8,128)S(1)} %select_maximum_fusion.own_in), channel_id=1, source_target_pairs={{0,28},{4,8},{8,4},{12,16},{16,12},{20,24},{24,20},{28,0},{1,29},{... | collective-permute-start | bytes 28520 | tf_op jit(solution)/shard_map/ppermute | solution.py:365
  7.4 0.7 %collective-permute-start.2 = (f32[33,72]{1,0:T(8,128)S(1)}, f32[33,72]{1,0:T(8,128)S(1)}, u32[]{:S(2)}, u32[]{:S(2)}) collective-permute-start(f32[33,72]{1,0:T(8,128)S(1)} %select_maximum_fusion.own_in), channel_id=1, source_target_pairs={{0,3},{1,2},{2,1},{3,0},{4,7},{5,6},{6,5},{7,4},{8,11},{9,10},{10,... | collective-permute-start | bytes 28520 | tf_op jit(solution)/shard_map/ppermute | solution.py:365
  8.0 0.0 collective-permute-start.1
  8.1 1.0 %collective-permute-start = (f32[33,72]{1,0:T(8,128)S(1)}, f32[33,72]{1,0:T(8,128)S(1)}, u32[]{:S(2)}, u32[]{:S(2)}) collective-permute-start(f32[33,72]{1,0:T(8,128)S(1)} %select_maximum_fusion.own_in), channel_id=1, source_target_pairs={{0,1},{1,0},{2,3},{3,2},{4,5},{5,4},{6,7},{7,6},{8,9},{9,8},{10,11... | collective-permute-start | bytes 28520 | tf_op jit(solution)/shard_map/ppermute | solution.py:365
  9.0 0.1 collective-permute-done.3.elem_b_in
  9.1 0.0 copy-start.2
  9.1 1.6 %collective-permute-done.2.band_b_in = f32[33,72]{1,0:T(8,128)S(1)} collective-permute-done((f32[33,72]{1,0:T(8,128)S(1)}, f32[33,72]{1,0:T(8,128)S(1)}, u32[]{:S(2)}, u32[]{:S(2)}) %collective-permute-start.2) | collective-permute-done | bytes 9536 | tf_op jit(solution)/shard_map/ppermute | solution.py:365
  10.7 0.0 copy-start.3
  10.7 1.3 %collective-permute-done.1.elem_a_in = f32[33,72]{1,0:T(8,128)S(1)} collective-permute-done((f32[33,72]{1,0:T(8,128)S(1)}, f32[33,72]{1,0:T(8,128)S(1)}, u32[]{:S(2)}, u32[]{:S(2)}) %collective-permute-start.1) | collective-permute-done | bytes 9536 | tf_op jit(solution)/shard_map/ppermute | solution.py:365
  12.0 0.0 copy-start.4
  12.0 0.0 collective-permute-done.band_a_in
  12.0 0.0 copy-start.5
  12.0 0.0 copy-done.1
  12.1 0.0 copy-done.2
  12.1 0.0 copy-done.3
  12.1 0.6 %copy-done.4 = f32[33,72]{1,0:T(8,128)} copy-done((f32[33,72]{1,0:T(8,128)}, f32[33,72]{1,0:T(8,128)S(1)}, u32[]{:S(2)}) %copy-start.4) | copy-done | bytes 9528
  12.6 0.0 copy-done.5
  12.6 10.7 %cloud_windows.1 = (bf16[6,32,3840]{2,1,0:T(8,128)(2,1)}, f32[32,72]{1,0:T(8,128)}, f32[32,128]{1,0:T(8,128)}) custom-call(bf16[6,32,3840]{2,1,0:T(8,128)(2,1)} %bitcast.13, f32[33,72]{1,0:T(8,128)} %copy-done.1, f32[33,72]{1,0:T(8,128)} %copy-done.5, f32[33,72]{1,0:T(8,128)} %copy-done.4, f32[33,72]{1,0:T(8,128)} %copy-done.3, f32[33,72]{1,0:T(8,128)} %copy-done.2, ...), custom_call_target="tpu_custom_call" | custom-call | tf_op jit(solution)/shard_map/cloud_windows/pallas_call | solution.py:383
  23.4 1.3 %collective-permute-start.7 = (f32[32,72]{1,0:T(8,128)}, f32[32,72]{1,0:T(8,128)S(1)}, u32[]{:S(2)}, u32[]{:S(2)}) collective-permute-start(f32[32,72]{1,0:T(8,128)} %get-tuple-element.7), channel_id=1, source_target_pairs={{0,28},{4,8},{8,4},{12,16},{16,12},{20,24},{24,20},{28,0},{1,29},{... | collective-permute-start | bytes 27656 | tf_op jit(solution)/shard_map/ppermute | solution.py:365
  24.6 0.9 %collective-permute-start.6 = (f32[32,72]{1,0:T(8,128)}, f32[32,72]{1,0:T(8,128)S(1)}, u32[]{:S(2)}, u32[]{:S(2)}) collective-permute-start(f32[32,72]{1,0:T(8,128)} %get-tuple-element.7), channel_id=1, source_target_pairs={{0,3},{1,2},{2,1},{3,0},{4,7},{5,6},{6,5},{7,4},{8,11},{9,10},{10,... | collective-permute-start | bytes 27656 | tf_op jit(solution)/shard_map/ppermute | solution.py:365
  25.5 0.4 %collective-permute-start.5 = (f32[32,72]{1,0:T(8,128)}, f32[32,72]{1,0:T(8,128)S(1)}, u32[]{:S(2)}, u32[]{:S(2)}) collective-permute-start(f32[32,72]{1,0:T(8,128)} %get-tuple-element.7), channel_id=1, source_target_pairs={{0,4},{4,0},{8,12},{12,8},{16,20},{20,16},{24,28},{28,24},{1,5},{5... | collective-permute-start | bytes 27656 | tf_op jit(solution)/shard_map/ppermute | solution.py:365
  25.9 1.2 %collective-permute-start.4 = (f32[32,72]{1,0:T(8,128)}, f32[32,72]{1,0:T(8,128)S(1)}, u32[]{:S(2)}, u32[]{:S(2)}) collective-permute-start(f32[32,72]{1,0:T(8,128)} %get-tuple-element.7), channel_id=1, source_target_pairs={{0,1},{1,0},{2,3},{3,2},{4,5},{5,4},{6,7},{7,6},{8,9},{9,8},{10,11... | collective-permute-start | bytes 27656 | tf_op jit(solution)/shard_map/ppermute | solution.py:365
  27.1 3.1 %collective-permute-done.7.elem_b = f32[32,72]{1,0:T(8,128)S(1)} collective-permute-done((f32[32,72]{1,0:T(8,128)}, f32[32,72]{1,0:T(8,128)S(1)}, u32[]{:S(2)}, u32[]{:S(2)}) %collective-permute-start.7) | collective-permute-done | bytes 9248 | tf_op jit(solution)/shard_map/ppermute | solution.py:365
  30.2 0.0 collective-permute-done.6.band_b
  30.2 0.0 collective-permute-done.5.elem_a
  30.2 0.0 collective-permute-done.4.band_a
  30.2 0.0 copy-start
  30.2 0.7 %copy-done = f32[32,128]{1,0:T(8,128)S(1)} copy-done((f32[32,128]{1,0:T(8,128)S(1)}, f32[32,128]{1,0:T(8,128)}, u32[]{:S(2)}) %copy-start) | copy-done | bytes 16408
  30.9 0.7 %host_section.1 = f32[32,72]{1,0:T(8,128)} custom-call(f32[32,128]{1,0:T(8,128)S(1)} %copy-done, f32[32,72]{1,0:T(8,128)S(1)} %collective-permute-done.4.band_a, f32[32,72]{1,0:T(8,128)S(1)} %collective-permute-done.5.elem_a, f32[32,72]{1,0:T(8,128)S(1)} %collective-permute-done.6.band_b, f32[32,72]{1,0:T(8,128)S(1)} %collective-permute-done.7.elem_b), custom_call_target="tpu_custom_call" | custom-call | tf_op jit(solution)/shard_map/host_section/pallas_call | solution.py:420
Async XLA Ops:
  1.4 10.7 %copy-start.1 = (f32[33,72]{1,0:T(8,128)}, f32[33,72]{1,0:T(8,128)S(1)}, u32[]{:S(2)}) copy-start(f32[33,72]{1,0:T(8,128)S(1)} %select_maximum_fusion.own_in) | copy-start | bytes 28516
  1.4 7.8 %collective-permute-start.3 = (f32[33,72]{1,0:T(8,128)S(1)}, f32[33,72]{1,0:T(8,128)S(1)}, u32[]{:S(2)}, u32[]{:S(2)}) collective-permute-start(f32[33,72]{1,0:T(8,128)S(1)} %select_maximum_fusion.own_in), channel_id=1, source_target_pairs={{0,28},{4,8},{8,4},{12,16},{16,12},{20,24},{24,20},{28,0},{1,29},{... | collective-permute-start | bytes 28520 | tf_op jit(solution)/shard_map/ppermute | solution.py:365
  7.4 3.4 %collective-permute-start.2 = (f32[33,72]{1,0:T(8,128)S(1)}, f32[33,72]{1,0:T(8,128)S(1)}, u32[]{:S(2)}, u32[]{:S(2)}) collective-permute-start(f32[33,72]{1,0:T(8,128)S(1)} %select_maximum_fusion.own_in), channel_id=1, source_target_pairs={{0,3},{1,2},{2,1},{3,0},{4,7},{5,6},{6,5},{7,4},{8,11},{9,10},{10,... | collective-permute-start | bytes 28520 | tf_op jit(solution)/shard_map/ppermute | solution.py:365
  8.0 4.0 %collective-permute-start.1 = (f32[33,72]{1,0:T(8,128)S(1)}, f32[33,72]{1,0:T(8,128)S(1)}, u32[]{:S(2)}, u32[]{:S(2)}) collective-permute-start(f32[33,72]{1,0:T(8,128)S(1)} %select_maximum_fusion.own_in), channel_id=1, source_target_pairs={{0,4},{4,0},{8,12},{12,8},{16,20},{20,16},{24,28},{28,24},{1,5},{5... | collective-permute-start | bytes 28520 | tf_op jit(solution)/shard_map/ppermute | solution.py:365
  8.1 4.0 %collective-permute-start = (f32[33,72]{1,0:T(8,128)S(1)}, f32[33,72]{1,0:T(8,128)S(1)}, u32[]{:S(2)}, u32[]{:S(2)}) collective-permute-start(f32[33,72]{1,0:T(8,128)S(1)} %select_maximum_fusion.own_in), channel_id=1, source_target_pairs={{0,1},{1,0},{2,3},{3,2},{4,5},{5,4},{6,7},{7,6},{8,9},{9,8},{10,11... | collective-permute-start | bytes 28520 | tf_op jit(solution)/shard_map/ppermute | solution.py:365
  9.1 2.9 %copy-start.2 = (f32[33,72]{1,0:T(8,128)}, f32[33,72]{1,0:T(8,128)S(1)}, u32[]{:S(2)}) copy-start(f32[33,72]{1,0:T(8,128)S(1)} %collective-permute-done.3.elem_b_in) | copy-start | bytes 28516
  10.7 1.3 %copy-start.3 = (f32[33,72]{1,0:T(8,128)}, f32[33,72]{1,0:T(8,128)S(1)}, u32[]{:S(2)}) copy-start(f32[33,72]{1,0:T(8,128)S(1)} %collective-permute-done.2.band_b_in) | copy-start | bytes 28516
  12.0 0.6 %copy-start.4 = (f32[33,72]{1,0:T(8,128)}, f32[33,72]{1,0:T(8,128)S(1)}, u32[]{:S(2)}) copy-start(f32[33,72]{1,0:T(8,128)S(1)} %collective-permute-done.1.elem_a_in) | copy-start | bytes 28516
  12.0 0.6 %copy-start.5 = (f32[33,72]{1,0:T(8,128)}, f32[33,72]{1,0:T(8,128)S(1)}, u32[]{:S(2)}) copy-start(f32[33,72]{1,0:T(8,128)S(1)} %collective-permute-done.band_a_in) | copy-start | bytes 28516
  23.4 6.8 %collective-permute-start.7 = (f32[32,72]{1,0:T(8,128)}, f32[32,72]{1,0:T(8,128)S(1)}, u32[]{:S(2)}, u32[]{:S(2)}) collective-permute-start(f32[32,72]{1,0:T(8,128)} %get-tuple-element.7), channel_id=1, source_target_pairs={{0,28},{4,8},{8,4},{12,16},{16,12},{20,24},{24,20},{28,0},{1,29},{... | collective-permute-start | bytes 27656 | tf_op jit(solution)/shard_map/ppermute | solution.py:365
  24.6 5.6 %collective-permute-start.6 = (f32[32,72]{1,0:T(8,128)}, f32[32,72]{1,0:T(8,128)S(1)}, u32[]{:S(2)}, u32[]{:S(2)}) collective-permute-start(f32[32,72]{1,0:T(8,128)} %get-tuple-element.7), channel_id=1, source_target_pairs={{0,3},{1,2},{2,1},{3,0},{4,7},{5,6},{6,5},{7,4},{8,11},{9,10},{10,... | collective-permute-start | bytes 27656 | tf_op jit(solution)/shard_map/ppermute | solution.py:365
  25.5 4.7 %collective-permute-start.5 = (f32[32,72]{1,0:T(8,128)}, f32[32,72]{1,0:T(8,128)S(1)}, u32[]{:S(2)}, u32[]{:S(2)}) collective-permute-start(f32[32,72]{1,0:T(8,128)} %get-tuple-element.7), channel_id=1, source_target_pairs={{0,4},{4,0},{8,12},{12,8},{16,20},{20,16},{24,28},{28,24},{1,5},{5... | collective-permute-start | bytes 27656 | tf_op jit(solution)/shard_map/ppermute | solution.py:365
  25.9 4.3 %collective-permute-start.4 = (f32[32,72]{1,0:T(8,128)}, f32[32,72]{1,0:T(8,128)S(1)}, u32[]{:S(2)}, u32[]{:S(2)}) collective-permute-start(f32[32,72]{1,0:T(8,128)} %get-tuple-element.7), channel_id=1, source_target_pairs={{0,1},{1,0},{2,3},{3,2},{4,5},{5,4},{6,7},{7,6},{8,9},{9,8},{10,11... | collective-permute-start | bytes 27656 | tf_op jit(solution)/shard_map/ppermute | solution.py:365
  30.2 0.7 %copy-start = (f32[32,128]{1,0:T(8,128)S(1)}, f32[32,128]{1,0:T(8,128)}, u32[]{:S(2)}) copy-start(f32[32,128]{1,0:T(8,128)} %get-tuple-element.6.aux) | copy-start | bytes 49156
where the time goes:
time: 32.2 us; the launch traced here: 31.6 us
  starting transfers between devices  11.4 us (35%)
  Pallas kernels  11.4 us (35%)
  waiting for transfers between devices  6.13 us (19%)
  local copies, waits for them, and re-layouts  1.3 us (4%)
  other arithmetic  0.74 us (2%)
  between operations  0.68 us (2%)
    ppermute x8, starting transfers between devices, neighbours(): found.append(lax.ppermute(block, axis, pairs))  11.4 us
    pallas_call x1, Pallas kernels, body(): pl.pallas_call(cloud_kernel, out_shape=(jax.ShapeDtypeStruct(cloud.shape,...  10.7 us
    ppermute x8, waiting for transfers between devices, neighbours(): found.append(lax.ppermute(block, axis, pairs))  6.13 us
    unnamed x12, local copies, waits for them, and re-layouts  1.3 us
    concatenate x1, other arithmetic, body(): jnp.concatenate([host, jnp.pad(kappa, ((0, 0), (0, levels - COLS)))], axi...  0.74 us
    pallas_call x1, Pallas kernels, body(): pl.pallas_call(host_kernel, out_shape=jax.ShapeDtypeStruct((COLS, levels)...  0.69 us
  transfers between devices with their start and end apart: 8, of which 4 were waited for; matrix products, arithmetic and copies ran while one was open for 0% of the time, Pallas kernels for 0%

commit v1 on v0

--- a/solution.py
+++ b/solution.py
@@ -18,7 +18,7 @@
 QUARTER = NZC // 4
 HALF_TILES = NZC // 4
 CELLS = NZC * NXC
-CHUNK = 3
+CHUNK = 5
 CLOUD_STEP = 0.1
 F32 = jnp.float32
 BF16 = jnp.bfloat16
@@ -167,9 +167,9 @@
             diffs[:, place * LANES : (place + 1) * LANES] = rows.astype(BF16)
 
 
-def tendency(diffs, backx, to_column):
+def tendency(diffs, backx):
     both = jnp.dot(diffs[...], backx[...], preferred_element_type=F32)
-    return permuted(to_column, both[:, :LANES] + both[:, LANES:])
+    return both[:, :LANES] + both[:, LANES:]
 
 
 def swapped_halves(low, one, two):
@@ -179,19 +179,19 @@
 
 
 def cloud_kernel(
-    cloud_in, own_in, band_a_in, elem_a_in, band_b_in, elem_b_in, counts_in, level_in, back_in, coup_in, fscale_in,
+    cloud_in, own_in, band_a_in, elem_b_in, elem_a_in, band_b_in, counts_in, level_in, back_in, coup_in, fscale_in,
     bweight_in,
     cloud_out, host_out, aux_out,
-    own, band_a, elem_a, band_b, elem_b, counts, level_map, back_t, coup, fscale, bweight,
+    own, band_a, elem_b, elem_a, band_b, counts, level_map, back_t, coup, fscale, bweight,
     state, force, sums, edge, dmat, cmat, counts16, backx, diffs, most, expand,
     out_buf, cloud, host_buf, aux, sems,
 ):
     levels = host_out.shape[1]
     sources = (
-        own_in, band_a_in, elem_a_in, band_b_in, elem_b_in, counts_in, level_in, back_in, coup_in, fscale_in,
+        own_in, band_a_in, elem_b_in, elem_a_in, band_b_in, counts_in, level_in, back_in, coup_in, fscale_in,
         bweight_in,
     )
-    places = (own, band_a, elem_a, band_b, elem_b, counts, level_map, back_t, coup, fscale, bweight)
+    places = (own, band_a, elem_b, elem_a, band_b, counts, level_map, back_t, coup, fscale, bweight)
     copies = [
         pltpu.make_async_copy(src, dst, sems.at[FIELDS + i])
         for i, (src, dst) in enumerate(zip(sources, places))
@@ -270,7 +270,9 @@
         jnp.concatenate([south[COLS - 1 : COLS], host[:-1]], axis=0) - host
     )
 
-    prepare_force(force, permuted(to_slot, host), level_map, fscale, expand)
+    host_sorted = permuted(to_slot, host)
+    prepare_force(force, host_sorted, level_map, fscale, expand)
+    spread_sorted = permuted(to_slot, spread)
 
     low = lane_iota(COLS, LANES) < NXC
     for copy in loads:
@@ -293,12 +295,14 @@
 
     advance_window(state, force, counts16, most, edge, dmat, cmat)
     differences(state, sums, weights, diffs)
-    tend = tendency(diffs, backx, to_column)
+    tend_sorted = tendency(diffs, backx)
+    host_sorted = host_sorted + (tend_sorted[:, :levels] + spread_sorted)
+    prepare_force(force, host_sorted, level_map, fscale, expand)
+    tend = permuted(to_column, tend_sorted)
     host = host + (tend[:, :levels] + spread)
     host_buf[...] = host
     sending = [pltpu.make_async_copy(host_buf, host_out, sems.at[0])]
     sending[0].start()
-    prepare_force(force, permuted(to_slot, host), level_map, fscale, expand)
     advance_window(state, force, counts16, most, edge, dmat, cmat)
     for fields in (range(0, FIELDS // 2), range(FIELDS // 2, FIELDS)):
         for tile in range(HALF_TILES):
@@ -330,7 +334,7 @@
             sending.append(copy)
     differences(state, sums, weights, diffs)
 
-    tend = tendency(diffs, backx, to_column)
+    tend = permuted(to_column, tendency(diffs, backx))
     zero = jnp.zeros((1, levels), F32)
     base = host + (tend[:, :levels] - (face_a + face_b + face_n + face_s) * host)
     base = base + face_n * jnp.concatenate([host[1:], zero], axis=0)
@@ -379,7 +383,8 @@
     cloud = jnp.transpose(crm_state[0], (1, 0, 2))
     host = jnp.transpose(host_state[:, 0, :], (1, 0))
     own = jnp.concatenate([host, jnp.pad(kappa, ((0, 0), (0, levels - COLS)))], axis=0)
-    near = neighbours(own)
+    band_a, elem_a, band_b, elem_b = neighbours(own)
+    near = (band_a, elem_b, elem_a, band_b)
     cloud_out, host, aux = pl.pallas_call(
         cloud_kernel,
         out_shape=(

time: 32.2 us -> 34.1 us (1.059); the launches traced: 31.6 us -> 34 us
  Pallas kernels: 11.4 us -> 14.1 us
  starting transfers between devices: 11.4 us -> 9.73 us
  waiting for transfers between devices: 6.13 us -> 7.37 us
    pallas_call x1, Pallas kernels: 10.7 us -> 13.5 us  [body(): pl.pallas_call(cloud_kernel, out_shape=(jax.ShapeDtypeStruct(cloud.shape,...]
    ppermute x8, starting transfers between devices: 11.4 us -> 9.73 us  [neighbours(): found.append(lax.ppermute(block, axis, pairs))]
    ppermute x8, waiting for transfers between devices: 6.13 us -> 7.37 us  [neighbours(): found.append(lax.ppermute(block, axis, pairs))]
  transfers between devices with their start and end apart: 8 -> 8, of which waited for: 4 -> 2; matrix products, arithmetic and copies ran while one was open for 0% -> 0% of each run, Pallas kernels for 0% -> 0%
where the time goes in v1:
time: 34.1 us; the launch traced here: 34 us
  Pallas kernels  14.1 us (41%)
  starting transfers between devices  9.73 us (29%)
  waiting for transfers between devices  7.37 us (22%)
  local copies, waits for them, and re-layouts  1.3 us (4%)
  other arithmetic  0.74 us (2%)
  between operations  0.69 us (2%)
    pallas_call x1, Pallas kernels, body(): pl.pallas_call(cloud_kernel, out_shape=(jax.ShapeDtypeStruct(cloud.shape,...  13.5 us
    ppermute x8, starting transfers between devices, neighbours(): found.append(lax.ppermute(block, axis, pairs))  9.73 us
    ppermute x8, waiting for transfers between devices, neighbours(): found.append(lax.ppermute(block, axis, pairs))  7.37 us
    unnamed x12, local copies, waits for them, and re-layouts  1.3 us
    concatenate x1, other arithmetic, body(): jnp.concatenate([host, jnp.pad(kappa, ((0, 0), (0, levels - COLS)))], axi...  0.74 us
    pallas_call x1, Pallas kernels, body(): pl.pallas_call(host_kernel, out_shape=jax.ShapeDtypeStruct((COLS, levels)...  0.69 us
  transfers between devices with their start and end apart: 8, of which 2 were waited for; matrix products, arithmetic and copies ran while one was open for 0% of the time, Pallas kernels for 0%

profile of v1, /device:TPU:0, one launch (start us, length us, event | category | flops | bytes accessed | tf_op | source)
XLA Modules:
  0.0 34.0 jit_solution(14238603921103073867)
XLA Ops:
  0.6 0.7 %select_maximum_fusion.own_in = f32[33,72]{1,0:T(8,128)S(1)} fusion(f32[1,32]{1,0:T(1,128)} %param.11, f32[32,72]{1,0:T(8,128)} %bitcast.15), kind=kLoop, calls=%fused_computation | loop fusion | flops 7128 | bytes 18848 | tf_op jit(solution)/shard_map/concatenate | solution.py:385
  1.4 0.0 copy-start.1
  1.4 2.4 %collective-permute-start.3 = (f32[33,72]{1,0:T(8,128)S(1)}, f32[33,72]{1,0:T(8,128)S(1)}, u32[]{:S(2)}, u32[]{:S(2)}) collective-permute-start(f32[33,72]{1,0:T(8,128)S(1)} %select_maximum_fusion.own_in), channel_id=1, source_target_pairs={{0,3},{1,2},{2,1},{3,0},{4,7},{5,6},{6,5},{7,4},{8,11},{9,10},{10,... | collective-permute-start | bytes 28520 | tf_op jit(solution)/shard_map/ppermute | solution.py:369
  3.8 1.5 %collective-permute-start.2 = (f32[33,72]{1,0:T(8,128)S(1)}, f32[33,72]{1,0:T(8,128)S(1)}, u32[]{:S(2)}, u32[]{:S(2)}) collective-permute-start(f32[33,72]{1,0:T(8,128)S(1)} %select_maximum_fusion.own_in), channel_id=1, source_target_pairs={{0,4},{4,0},{8,12},{12,8},{16,20},{20,16},{24,28},{28,24},{1,5},{5... | collective-permute-start | bytes 28520 | tf_op jit(solution)/shard_map/ppermute | solution.py:369
  5.3 3.6 %collective-permute-start.1 = (f32[33,72]{1,0:T(8,128)S(1)}, f32[33,72]{1,0:T(8,128)S(1)}, u32[]{:S(2)}, u32[]{:S(2)}) collective-permute-start(f32[33,72]{1,0:T(8,128)S(1)} %select_maximum_fusion.own_in), channel_id=1, source_target_pairs={{0,28},{4,8},{8,4},{12,16},{16,12},{20,24},{24,20},{28,0},{1,29},{... | collective-permute-start | bytes 28520 | tf_op jit(solution)/shard_map/ppermute | solution.py:369
  8.9 0.1 collective-permute-start
  9.0 0.0 collective-permute-done.3.band_b_in
  9.0 0.0 copy-start.2
  9.0 0.0 collective-permute-done.2.elem_a_in
  9.0 0.0 copy-start.3
  9.0 2.7 %collective-permute-done.1.elem_b_in = f32[33,72]{1,0:T(8,128)S(1)} collective-permute-done((f32[33,72]{1,0:T(8,128)S(1)}, f32[33,72]{1,0:T(8,128)S(1)}, u32[]{:S(2)}, u32[]{:S(2)}) %collective-permute-start.1) | collective-permute-done | bytes 9536 | tf_op jit(solution)/shard_map/ppermute | solution.py:369
  11.8 0.0 copy-start.4
  11.8 0.0 collective-permute-done.band_a_in
  11.8 0.0 copy-start.5
  11.8 0.0 copy-done.1
  11.8 0.0 copy-done.2
  11.8 0.0 copy-done.3
  11.8 0.6 %copy-done.4 = f32[33,72]{1,0:T(8,128)} copy-done((f32[33,72]{1,0:T(8,128)}, f32[33,72]{1,0:T(8,128)S(1)}, u32[]{:S(2)}) %copy-start.4) | copy-done | bytes 9528
  12.4 0.0 copy-done.5
  12.4 13.5 %cloud_windows.1 = (bf16[6,32,3840]{2,1,0:T(8,128)(2,1)}, f32[32,72]{1,0:T(8,128)}, f32[32,128]{1,0:T(8,128)}) custom-call(bf16[6,32,3840]{2,1,0:T(8,128)(2,1)} %bitcast.13, f32[33,72]{1,0:T(8,128)} %copy-done.1, f32[33,72]{1,0:T(8,128)} %copy-done.5, f32[33,72]{1,0:T(8,128)} %copy-done.4, f32[33,72]{1,0:T(8,128)} %copy-done.3, f32[33,72]{1,0:T(8,128)} %copy-done.2, ...), custom_call_target="tpu_custom_call" | custom-call | tf_op jit(solution)/shard_map/cloud_windows/pallas_call | solution.py:388
  25.9 1.3 %collective-permute-start.7 = (f32[32,72]{1,0:T(8,128)}, f32[32,72]{1,0:T(8,128)S(1)}, u32[]{:S(2)}, u32[]{:S(2)}) collective-permute-start(f32[32,72]{1,0:T(8,128)} %get-tuple-element.7), channel_id=1, source_target_pairs={{0,28},{4,8},{8,4},{12,16},{16,12},{20,24},{24,20},{28,0},{1,29},{... | collective-permute-start | bytes 27656 | tf_op jit(solution)/shard_map/ppermute | solution.py:369
  27.2 0.0 collective-permute-start.6
  27.2 0.0 collective-permute-start.5
  27.2 0.8 %collective-permute-start.4 = (f32[32,72]{1,0:T(8,128)}, f32[32,72]{1,0:T(8,128)S(1)}, u32[]{:S(2)}, u32[]{:S(2)}) collective-permute-start(f32[32,72]{1,0:T(8,128)} %get-tuple-element.7), channel_id=1, source_target_pairs={{0,1},{1,0},{2,3},{3,2},{4,5},{5,4},{6,7},{7,6},{8,9},{9,8},{10,11... | collective-permute-start | bytes 27656 | tf_op jit(solution)/shard_map/ppermute | solution.py:369
  27.9 4.6 %collective-permute-done.7.elem_b = f32[32,72]{1,0:T(8,128)S(1)} collective-permute-done((f32[32,72]{1,0:T(8,128)}, f32[32,72]{1,0:T(8,128)S(1)}, u32[]{:S(2)}, u32[]{:S(2)}) %collective-permute-start.7) | collective-permute-done | bytes 9248 | tf_op jit(solution)/shard_map/ppermute | solution.py:369
  32.6 0.0 collective-permute-done.6.band_b
  32.6 0.0 collective-permute-done.5.elem_a
  32.6 0.0 collective-permute-done.4.band_a
  32.6 0.0 copy-start
  32.6 0.7 %copy-done = f32[32,128]{1,0:T(8,128)S(1)} copy-done((f32[32,128]{1,0:T(8,128)S(1)}, f32[32,128]{1,0:T(8,128)}, u32[]{:S(2)}) %copy-start) | copy-done | bytes 16408
  33.3 0.7 %host_section.1 = f32[32,72]{1,0:T(8,128)} custom-call(f32[32,128]{1,0:T(8,128)S(1)} %copy-done, f32[32,72]{1,0:T(8,128)S(1)} %collective-permute-done.4.band_a, f32[32,72]{1,0:T(8,128)S(1)} %collective-permute-done.5.elem_a, f32[32,72]{1,0:T(8,128)S(1)} %collective-permute-done.6.band_b, f32[32,72]{1,0:T(8,128)S(1)} %collective-permute-done.7.elem_b), custom_call_target="tpu_custom_call" | custom-call | tf_op jit(solution)/shard_map/host_section/pallas_call | solution.py:425
Async XLA Ops:
  1.4 10.4 %copy-start.1 = (f32[33,72]{1,0:T(8,128)}, f32[33,72]{1,0:T(8,128)S(1)}, u32[]{:S(2)}) copy-start(f32[33,72]{1,0:T(8,128)S(1)} %select_maximum_fusion.own_in) | copy-start | bytes 28516
  1.4 7.6 %collective-permute-start.3 = (f32[33,72]{1,0:T(8,128)S(1)}, f32[33,72]{1,0:T(8,128)S(1)}, u32[]{:S(2)}, u32[]{:S(2)}) collective-permute-start(f32[33,72]{1,0:T(8,128)S(1)} %select_maximum_fusion.own_in), channel_id=1, source_target_pairs={{0,3},{1,2},{2,1},{3,0},{4,7},{5,6},{6,5},{7,4},{8,11},{9,10},{10,... | collective-permute-start | bytes 28520 | tf_op jit(solution)/shard_map/ppermute | solution.py:369
  3.8 5.2 %collective-permute-start.2 = (f32[33,72]{1,0:T(8,128)S(1)}, f32[33,72]{1,0:T(8,128)S(1)}, u32[]{:S(2)}, u32[]{:S(2)}) collective-permute-start(f32[33,72]{1,0:T(8,128)S(1)} %select_maximum_fusion.own_in), channel_id=1, source_target_pairs={{0,4},{4,0},{8,12},{12,8},{16,20},{20,16},{24,28},{28,24},{1,5},{5... | collective-permute-start | bytes 28520 | tf_op jit(solution)/shard_map/ppermute | solution.py:369
  5.3 6.5 %collective-permute-start.1 = (f32[33,72]{1,0:T(8,128)S(1)}, f32[33,72]{1,0:T(8,128)S(1)}, u32[]{:S(2)}, u32[]{:S(2)}) collective-permute-start(f32[33,72]{1,0:T(8,128)S(1)} %select_maximum_fusion.own_in), channel_id=1, source_target_pairs={{0,28},{4,8},{8,4},{12,16},{16,12},{20,24},{24,20},{28,0},{1,29},{... | collective-permute-start | bytes 28520 | tf_op jit(solution)/shard_map/ppermute | solution.py:369
  8.9 2.9 %collective-permute-start = (f32[33,72]{1,0:T(8,128)S(1)}, f32[33,72]{1,0:T(8,128)S(1)}, u32[]{:S(2)}, u32[]{:S(2)}) collective-permute-start(f32[33,72]{1,0:T(8,128)S(1)} %select_maximum_fusion.own_in), channel_id=1, source_target_pairs={{0,1},{1,0},{2,3},{3,2},{4,5},{5,4},{6,7},{7,6},{8,9},{9,8},{10,11... | collective-permute-start | bytes 28520 | tf_op jit(solution)/shard_map/ppermute | solution.py:369
  9.0 2.8 %copy-start.2 = (f32[33,72]{1,0:T(8,128)}, f32[33,72]{1,0:T(8,128)S(1)}, u32[]{:S(2)}) copy-start(f32[33,72]{1,0:T(8,128)S(1)} %collective-permute-done.3.band_b_in) | copy-start | bytes 28516
  9.0 2.8 %copy-start.3 = (f32[33,72]{1,0:T(8,128)}, f32[33,72]{1,0:T(8,128)S(1)}, u32[]{:S(2)}) copy-start(f32[33,72]{1,0:T(8,128)S(1)} %collective-permute-done.2.elem_a_in) | copy-start | bytes 28516
  11.8 0.6 %copy-start.4 = (f32[33,72]{1,0:T(8,128)}, f32[33,72]{1,0:T(8,128)S(1)}, u32[]{:S(2)}) copy-start(f32[33,72]{1,0:T(8,128)S(1)} %collective-permute-done.1.elem_b_in) | copy-start | bytes 28516
  11.8 0.6 %copy-start.5 = (f32[33,72]{1,0:T(8,128)}, f32[33,72]{1,0:T(8,128)S(1)}, u32[]{:S(2)}) copy-start(f32[33,72]{1,0:T(8,128)S(1)} %collective-permute-done.band_a_in) | copy-start | bytes 28516
  25.9 6.7 %collective-permute-start.7 = (f32[32,72]{1,0:T(8,128)}, f32[32,72]{1,0:T(8,128)S(1)}, u32[]{:S(2)}, u32[]{:S(2)}) collective-permute-start(f32[32,72]{1,0:T(8,128)} %get-tuple-element.7), channel_id=1, source_target_pairs={{0,28},{4,8},{8,4},{12,16},{16,12},{20,24},{24,20},{28,0},{1,29},{... | collective-permute-start | bytes 27656 | tf_op jit(solution)/shard_map/ppermute | solution.py:369
  27.2 5.4 %collective-permute-start.6 = (f32[32,72]{1,0:T(8,128)}, f32[32,72]{1,0:T(8,128)S(1)}, u32[]{:S(2)}, u32[]{:S(2)}) collective-permute-start(f32[32,72]{1,0:T(8,128)} %get-tuple-element.7), channel_id=1, source_target_pairs={{0,3},{1,2},{2,1},{3,0},{4,7},{5,6},{6,5},{7,4},{8,11},{9,10},{10,... | collective-permute-start | bytes 27656 | tf_op jit(solution)/shard_map/ppermute | solution.py:369
  27.2 5.4 %collective-permute-start.5 = (f32[32,72]{1,0:T(8,128)}, f32[32,72]{1,0:T(8,128)S(1)}, u32[]{:S(2)}, u32[]{:S(2)}) collective-permute-start(f32[32,72]{1,0:T(8,128)} %get-tuple-element.7), channel_id=1, source_target_pairs={{0,4},{4,0},{8,12},{12,8},{16,20},{20,16},{24,28},{28,24},{1,5},{5... | collective-permute-start | bytes 27656 | tf_op jit(solution)/shard_map/ppermute | solution.py:369
  27.2 5.4 %collective-permute-start.4 = (f32[32,72]{1,0:T(8,128)}, f32[32,72]{1,0:T(8,128)S(1)}, u32[]{:S(2)}, u32[]{:S(2)}) collective-permute-start(f32[32,72]{1,0:T(8,128)} %get-tuple-element.7), channel_id=1, source_target_pairs={{0,1},{1,0},{2,3},{3,2},{4,5},{5,4},{6,7},{7,6},{8,9},{9,8},{10,11... | collective-permute-start | bytes 27656 | tf_op jit(solution)/shard_map/ppermute | solution.py:369
  32.6 0.7 %copy-start = (f32[32,128]{1,0:T(8,128)S(1)}, f32[32,128]{1,0:T(8,128)}, u32[]{:S(2)}) copy-start(f32[32,128]{1,0:T(8,128)} %get-tuple-element.6.aux) | copy-start | bytes 49156
